TPU v7x, 32 devices: a whole 2x2x4 slice. The times are simulated.
32 devices in a mesh: dp: 4 (over z), frame: 2 (over x), row: 4 (over y, core).
Axes of the slice: x: 2, y: 2, z: 4, core: 2. Of those that a mesh axis runs over, the one named last changes fastest.
Arguments:
- clip_input: bfloat16 [4, 8, 16, 240, 128], P('dp', 'frame', 'row'), may hold values from -6 to 6
- cotangent: bfloat16 [4, 8, 16, 240, 128], P('dp', 'frame', 'row'), may hold values from -6 to 6
- spatial_weight: bfloat16 [3, 3, 128, 128], replicated, may hold values from -0.1875 to 0.1875
- temporal_weight: bfloat16 [3, 128, 128], replicated, may hold values from -0.3125 to 0.3125
Outputs:
- block_output: bfloat16 [4, 8, 16, 240, 128], P('dp', 'frame', 'row')
- input_grad: bfloat16 [4, 8, 16, 240, 128], P('dp', 'frame', 'row')
- weight_grads: float32 [1536, 128], P(('dp', 'frame', 'row'))
All inputs are finite; a program needn't handle non-finite values.
Results may differ from a plain program's by a relative error of at most 0.0045.
Values may be sent and summed in bfloat16 or wider, within the bound.
A program may use at most 64 MiB of HBM per device.

v0:
```python
import math

import jax
import jax.numpy as jnp
from jax import lax
from jax.sharding import PartitionSpec as P


def extended_2(shard, sides, width):
    for axis, dim in sides:
        peers, length = (lax.axis_size(axis), shard.shape[dim])
        up = [(i, (i + 1) % peers) for i in range(peers - 1)]
        down = [(j, i) for i, j in up]
        last = lax.slice_in_dim(shard, length - width, length, axis=dim)
        first = lax.slice_in_dim(shard, 0, width, axis=dim)
        before = lax.ppermute(last, axis, up)
        after = lax.ppermute(first, axis, down)
        shard = jnp.concatenate([before, shard, after], axis=dim)
    return shard


def spatial_taps(padded, weights, rows, cols):
    chans = padded.shape[-1]
    total = jnp.zeros((padded.shape[0] * rows * cols, weights.shape[-1]), jnp.float32)
    for i in range(3):
        for j in range(3):
            piece = padded[:, i : i + rows, j : j + cols, :].reshape(-1, chans)
            total = total + jnp.dot(piece, weights[i, j], preferred_element_type=jnp.float32)
    return total.reshape(padded.shape[0], rows, cols, -1)


def contract_rows(left, right):
    return lax.dot_general(
        left, right, (((0,), (0,)), ((), ())), preferred_element_type=jnp.float32
    )


def temporal_pass(earlier, act_now, grad_now, later, temporal_weight):
    frames = act_now.shape[0]
    chans = act_now.shape[-1]
    act_ext = jnp.concatenate([earlier, act_now], axis=0)
    grad_ext = jnp.concatenate([grad_now, later], axis=0)
    grad_flat = grad_now.reshape(-1, chans)
    mixed = jnp.zeros((grad_flat.shape[0], chans), jnp.float32)
    act_grad = jnp.zeros((grad_flat.shape[0], chans), jnp.float32)
    temporal_list = []
    for k in range(3):
        shifted = act_ext[2 - k : 2 - k + frames].reshape(-1, chans)
        mixed = mixed + jnp.dot(shifted, temporal_weight[k], preferred_element_type=jnp.float32)
        ahead = grad_ext[k : k + frames].reshape(-1, chans)
        act_grad = act_grad + jnp.dot(
            ahead, temporal_weight[k].T, preferred_element_type=jnp.float32
        )
        temporal_list.append(contract_rows(shifted, grad_flat))
    mixed = mixed.astype(jnp.bfloat16).reshape(act_now.shape)
    act_grad = act_grad.astype(jnp.bfloat16).reshape(act_now.shape)
    return (mixed, act_grad, jnp.concatenate(temporal_list, axis=0))


def on_device(clip_input, cotangent, spatial_weight, temporal_weight):
    frames = clip_input.shape[1]
    rows = clip_input.shape[2]
    cols = clip_input.shape[3]
    chans = clip_input.shape[4]
    cells = (
        lax.axis_size("dp") * frames * lax.axis_size("frame") * rows * lax.axis_size("row") * cols
    )
    scale = 1.0 / math.sqrt(cells)
    extended = extended_2(clip_input, (("row", 2),), 1)[0]
    xpad = jnp.pad(extended, ((0, 0), (0, 0), (1, 1), (0, 0)))
    pre = spatial_taps(xpad, spatial_weight, rows, cols)
    act = jax.nn.silu(pre).astype(jnp.bfloat16)
    grad_out = cotangent[0]
    act_band, grad_band = (
        lax.all_to_all(act[None], "frame", split_axis=3, concat_axis=1, tiled=True),
        lax.all_to_all(grad_out[None], "frame", split_axis=3, concat_axis=1, tiled=True),
    )
    act_band = act_band[0]
    grad_band = grad_band[0]
    edge_shape = (2,) + act_band.shape[1:]
    earlier = jnp.zeros(edge_shape, jnp.bfloat16)
    later = jnp.zeros(edge_shape, jnp.bfloat16)
    mixed_band, grad_act_band, temporal_terms = temporal_pass(
        earlier, act_band, grad_band, later, temporal_weight
    )
    mixed, act_grad = (
        lax.all_to_all(mixed_band[None], "frame", split_axis=1, concat_axis=3, tiled=True),
        lax.all_to_all(grad_act_band[None], "frame", split_axis=1, concat_axis=3, tiled=True),
    )
    mixed = mixed[0]
    act_grad = act_grad[0]
    block_output = (clip_input[0].astype(jnp.float32) + mixed.astype(jnp.float32)).astype(
        jnp.bfloat16
    )
    sigma = jax.nn.sigmoid(pre)
    pre_grad = (act_grad.astype(jnp.float32) * sigma * (1.0 + pre * (1.0 - sigma))).astype(
        jnp.bfloat16
    )
    pg_flat = pre_grad.reshape(-1, chans)
    spatial_list = []
    for i in range(3):
        for j in range(3):
            piece = xpad[:, i : i + rows, j : j + cols, :].reshape(-1, chans)
            spatial_list.append(contract_rows(piece, pg_flat))
    grad_ext = extended_2(pre_grad[None], (("row", 2),), 1)[0]
    gpad = jnp.pad(grad_ext, ((0, 0), (0, 0), (1, 1), (0, 0)))
    backward = jnp.zeros((frames * rows * cols, chans), jnp.float32)
    for i in range(3):
        for j in range(3):
            piece = gpad[:, 2 - i : 2 - i + rows, 2 - j : 2 - j + cols, :].reshape(-1, chans)
            backward = backward + jnp.dot(
                piece, spatial_weight[i, j].T, preferred_element_type=jnp.float32
            )
    input_grad = (grad_out.astype(jnp.float32).reshape(-1, chans) + backward).astype(jnp.bfloat16)
    input_grad = input_grad.reshape(clip_input.shape)
    partial_terms = jnp.concatenate(spatial_list + [temporal_terms], axis=0)
    summed = lax.psum_scatter(
        partial_terms, ("dp", "frame", "row"), scatter_dimension=0, tiled=True
    )
    return (block_output[None], input_grad, summed * scale)


def solution(mesh):
    placed = (P("dp", "frame", "row", None, None), P("dp", "frame", "row", None, None), P(), P())
    return jax.shard_map(
        on_device,
        mesh=mesh,
        in_specs=placed,
        out_specs=(
            P("dp", "frame", "row", None, None),
            P("dp", "frame", "row", None, None),
            P(("dp", "frame", "row"), None),
        ),
        check_vma=False,
    )
```

profile of v0, /device:TPU:1, one launch (start us, length us, event | category | flops | bytes accessed | tf_op | source)
XLA Modules:
  0.0 202.5 jit_solution(3033453957739052537)
XLA Ops:
  8.3 4.5 %collective-permute-start = (bf16[1,4,1,240,128]{4,3,2,1,0:T(8,128)(2,1)S(1)}, bf16[1,4,1,240,128]{4,3,2,1,0:T(8,128)(2,1)S(1)}, u32[]{:S(2)}, u32[]{:S(2)}) collective-permute-start(bf16[1,4,1,240,128]{4,3,2,1,0:T(8,128)(2,1)S(1)} %get-tuple-element.29), channel_id=1, source_target_pairs={{0,1},{1,2},{2,3},{4,5},{5,6},{6,7},{8,9},{9,10},{10,11},{12,13},{... | collective-permute-start | bytes 737288 | tf_op jit(solution)/shard_map/ppermute | solution.py:16
  12.8 2.1 %collective-permute-start.1 = (bf16[1,4,1,240,128]{4,3,2,1,0:T(8,128)(2,1)S(1)}, bf16[1,4,1,240,128]{4,3,2,1,0:T(8,128)(2,1)S(1)}, u32[]{:S(2)}, u32[]{:S(2)}) collective-permute-start(bf16[1,4,1,240,128]{4,3,2,1,0:T(8,128)(2,1)S(1)} %get-tuple-element.30), channel_id=1, source_target_pairs={{1,0},{2,1},{3,2},{5,4},{6,5},{7,6},{9,8},{10,9},{11,10},{13,12},{... | collective-permute-start | bytes 737288 | tf_op jit(solution)/shard_map/ppermute | solution.py:17
  14.9 2.5 %copy.31 = bf16[1,4,4,240,128]{4,2,1,0,3:T(4,128)(2,1)} copy(bf16[1,4,4,240,128]{4,3,2,1,0:T(8,128)(2,1)} %param.5) | data formatting | bytes 1966080 | tf_op args[1]
  17.4 4.4 %all-to-all-start.2 = ((bf16[1,4,4,240,128]{4,2,1,0,3:T(4,128)(2,1)}), bf16[1,4,4,240,128]{4,2,1,0,3:T(4,128)(2,1)}, u32[]{:S(2)}, u32[]{:S(2)}) async-start(bf16[1,4,4,240,128]{4,2,1,0,3:T(4,128)(2,1)} %copy.31), calls=%async_computation.2 | async-start | bytes 1966080 | tf_op jit(solution)/shard_map/all_to_all | solution.py:76
  23.4 3.7 %pad_slice_fusion.10 = (bf16[4,4,240,128]{3,2,1,0:T(8,128)(2,1)S(1)}, bf16[4,4,240,128]{3,2,1,0:T(8,128)(2,1)S(1)}, bf16[4,4,240,128]{3,2,1,0:T(8,128)(2,1)S(1)}...) fusion(bf16[4,6,240,128]{3,2,1,0:T(8,128)(2,1)S(1)} %maximum_bi, ...), kind=kLoop, calls=%fused_computation.69 | loop fusion | bytes 13271040 | tf_op jit(solution)/shard_map/slice | solution.py:27
  29.5 1.7 convolution_add_fusion.14
  31.2 1.9 all-to-all-done.2
  37.6 4.6 %all-to-all-start.3 = ((bf16[1,8,4,120,128]{4,3,2,0,1:T(8,128)(2,1)}), bf16[1,8,4,120,128]{4,3,2,0,1:T(8,128)(2,1)}, u32[]{:S(2)}, u32[]{:S(2)}) async-start(bf16[1,8,4,120,128]{4,3,2,0,1:T(8,128)(2,1)} %bitcast.270), calls=%async_computation.3 | async-start | bytes 1966080 | tf_op jit(solution)/shard_map/all_to_all | solution.py:88
  42.2 2.3 %convolution_add_fusion.13 = f32[3840,128]{1,0:T(8,128)S(1)} fusion(f32[3840,128]{1,0:T(8,128)} %convolution_add_fusion.14, bf16[3840,128]{1,0:T(8,128)(2,1)} %bitcast.254, bf16[3,3,128,128]{3,2,1,0:T(8,128)(2,1)} %param.6), kind=kOutput, calls=%fused_computation.14 | convolution fusion | flops 126320640 | bytes 4947968 | tf_op jit(solution)/shard_map/dot_general | solution.py:28
  44.5 2.5 %convolution_add_fusion.12 = f32[3840,128]{1,0:T(8,128)} fusion(f32[3840,128]{1,0:T(8,128)S(1)} %convolution_add_fusion.13, bf16[3840,128]{1,0:T(8,128)(2,1)S(1)} %bitcast.253, bf16[3,3,128,128]{3,2,1,0:T(8,128)(2,1)} %param.6), kind=kOutput, calls=%fused_computation.13 | convolution fusion | flops 126320640 | bytes 4947968 | tf_op jit(solution)/shard_map/dot_general | solution.py:28
  46.9 7.4 %all-to-all-done.3 = bf16[1,8,4,120,128]{4,3,2,0,1:T(8,128)(2,1)} async-done(((bf16[1,8,4,120,128]{4,3,2,0,1:T(8,128)(2,1)}), bf16[1,8,4,120,128]{4,3,2,0,1:T(8,128)(2,1)}, u32[]{:S(2)}, u32[]{:S(2)}) %all-to-all-start.3) | async-done | bytes 983072 | tf_op jit(solution)/shard_map/all_to_all | solution.py:88
  64.8 1.9 fusion.5
  68.0 4.4 %all-to-all-start = ((bf16[1,4,4,240,128]{4,2,1,0,3:T(4,128)(2,1)}), bf16[1,4,4,240,128]{4,2,1,0,3:T(4,128)(2,1)}, u32[]{:S(2)}, u32[]{:S(2)}) async-start(bf16[1,4,4,240,128]{4,2,1,0,3:T(4,128)(2,1)} %copy.26), calls=%async_computation | async-start | bytes 1966080 | tf_op jit(solution)/shard_map/all_to_all | solution.py:75
  73.6 3.5 %collective-permute-start.2 = (bf16[1,4,1,240,128]{4,3,2,1,0:T(8,128)(2,1)S(1)}, bf16[1,4,1,240,128]{4,3,2,1,0:T(8,128)(2,1)S(1)}, u32[]{:S(2)}, u32[]{:S(2)}) collective-permute-start(bf16[1,4,1,240,128]{4,3,2,1,0:T(8,128)(2,1)S(1)} %get-tuple-element.23), channel_id=1, source_target_pairs={{0,1},{1,2},{2,3},{4,5},{5,6},{6,7},{8,9},{9,10},{10,11},{12,13},{... | collective-permute-start | bytes 737288 | tf_op jit(solution)/shard_map/ppermute | solution.py:16
  77.2 2.1 %collective-permute-start.3 = (bf16[1,4,1,240,128]{4,3,2,1,0:T(8,128)(2,1)S(1)}, bf16[1,4,1,240,128]{4,3,2,1,0:T(8,128)(2,1)S(1)}, u32[]{:S(2)}, u32[]{:S(2)}) collective-permute-start(bf16[1,4,1,240,128]{4,3,2,1,0:T(8,128)(2,1)S(1)} %get-tuple-element.24), channel_id=1, source_target_pairs={{1,0},{2,1},{3,2},{5,4},{6,5},{7,6},{9,8},{10,9},{11,10},{13,12},{... | collective-permute-start | bytes 737288 | tf_op jit(solution)/shard_map/ppermute | solution.py:17
  79.3 2.4 %fusion.14 = f32[1536,128]{1,0:T(8,128)} fusion(f32[1536,128]{1,0:T(8,128)} %fusion.9, bf16[4,4,240,128]{3,2,1,0:T(8,128)(2,1)S(1)} %multiply_convert_fusion, bf16[1,4,1,240,128]{4,3,2,1,0:T(8,128)(2,1)} %copy-done.15, bf16[1,4,4,240,128]{4,3,2,1,0:T(8,128)(2,1)} %param.4, bf16[1,4,1,240,128]{4,3,2,1,0:T(8,128)(2,1)} %copy-done.13), kind=kOutput, calls=%fused_computation.56 | convolution fusion | flops 130252800 | bytes 2523136 | tf_op jit(solution)/shard_map/dot_general | solution.py:33
  82.8 2.3 %collective-permute-done.3 = bf16[1,4,1,240,128]{4,3,2,1,0:T(8,128)(2,1)S(1)} collective-permute-done((bf16[1,4,1,240,128]{4,3,2,1,0:T(8,128)(2,1)S(1)}, bf16[1,4,1,240,128]{4,3,2,1,0:T(8,128)(2,1)S(1)}, u32[]{:S(2)}, u32[]{:S(2)}) %collective-permute-start.3) | collective-permute-done | bytes 245792 | tf_op jit(solution)/shard_map/ppermute | solution.py:17
  85.3 3.9 %pad_slice_fusion.4 = (bf16[4,4,240,128]{3,2,1,0:T(8,128)(2,1)}, bf16[4,4,240,128]{3,2,1,0:T(8,128)(2,1)S(1)}, bf16[4,4,240,128]{3,2,1,0:T(8,128)(2,1)S(1)}, bf1...) fusion(bf16[4,6,240,128]{3,2,1,0:T(8,128)(2,1)S(1)} %maximum_bi, ...), kind=kLoop, calls=%fused_computation.63 | loop fusion | bytes 13271040 | tf_op jit(solution)/shard_map/slice | solution.py:110
  91.7 1.7 convolution_add_fusion.2
  94.9 2.7 %fusion.7 = f32[1536,128]{1,0:T(8,128)} fusion(f32[1536,128]{1,0:T(8,128)} %fusion.8, bf16[1,4,4,2,120,128]{5,2,1,4,3,0:T(4,128)(2,1)} %bitcast.35, bf16[1,4,4,2,120,128]{5,2,1,4,3,0:T(4,128)(2,1)} %bitcast.20), kind=kOutput, calls=%fused_computation.42 | convolution fusion | flops 125829120 | bytes 2031616 | tf_op jit(solution)/shard_map/dot_general | solution.py:33
  103.0 4.5 %all-to-all-start.1 = ((bf16[1,8,4,120,128]{4,3,2,0,1:T(8,128)(2,1)}), bf16[1,8,4,120,128]{4,3,2,0,1:T(8,128)(2,1)}, u32[]{:S(2)}, u32[]{:S(2)}) async-start(bf16[1,8,4,120,128]{4,3,2,0,1:T(8,128)(2,1)} %bitcast.271), calls=%async_computation.1 | async-start | bytes 1966080 | tf_op jit(solution)/shard_map/all_to_all | solution.py:87
  107.5 1.8 convolution_add_fusion.1
  110.7 6.5 %all-to-all-done.1 = bf16[1,8,4,120,128]{4,3,2,0,1:T(8,128)(2,1)} async-done(((bf16[1,8,4,120,128]{4,3,2,0,1:T(8,128)(2,1)}), bf16[1,8,4,120,128]{4,3,2,0,1:T(8,128)(2,1)}, u32[]{:S(2)}, u32[]{:S(2)}) %all-to-all-start.1) | async-done | bytes 983072 | tf_op jit(solution)/shard_map/all_to_all | solution.py:87
  121.0 73.3 %reduce-scatter.2.cloned.1.call-done = f32[48,128]{1,0:T(8,128)} async-done(((f32[1536,128]{1,0:T(8,128)}), f32[48,128]{1,0:T(8,128)}) %reduce-scatter.2.cloned.1.call-update) | async-done | bytes 24592 | tf_op jit(solution)/shard_map/reduce_scatter | solution.py:117
  (84 shorter events, 39.6 us)
Async XLA Ops:
  8.3 13.6 %collective-permute-start = (bf16[1,4,1,240,128]{4,3,2,1,0:T(8,128)(2,1)S(1)}, bf16[1,4,1,240,128]{4,3,2,1,0:T(8,128)(2,1)S(1)}, u32[]{:S(2)}, u32[]{:S(2)}) collective-permute-start(bf16[1,4,1,240,128]{4,3,2,1,0:T(8,128)(2,1)S(1)} %get-tuple-element.29), channel_id=1, source_target_pairs={{0,1},{1,2},{2,3},{4,5},{5,6},{6,7},{8,9},{9,10},{10,11},{12,13},{... | collective-permute-start | bytes 737288 | tf_op jit(solution)/shard_map/ppermute | solution.py:16
  12.8 10.4 %copy-start.5 = (bf16[1,4,4,240,128]{4,3,2,1,0:T(8,128)(2,1)S(1)}, bf16[1,4,4,240,128]{4,3,2,1,0:T(8,128)(2,1)}, u32[]{:S(2)}) copy-start(bf16[1,4,4,240,128]{4,3,2,1,0:T(8,128)(2,1)} %param.4) | copy-start | bytes 2949124
  12.8 9.0 %collective-permute-start.1 = (bf16[1,4,1,240,128]{4,3,2,1,0:T(8,128)(2,1)S(1)}, bf16[1,4,1,240,128]{4,3,2,1,0:T(8,128)(2,1)S(1)}, u32[]{:S(2)}, u32[]{:S(2)}) collective-permute-start(bf16[1,4,1,240,128]{4,3,2,1,0:T(8,128)(2,1)S(1)} %get-tuple-element.30), channel_id=1, source_target_pairs={{1,0},{2,1},{3,2},{5,4},{6,5},{7,6},{9,8},{10,9},{11,10},{13,12},{... | collective-permute-start | bytes 737288 | tf_op jit(solution)/shard_map/ppermute | solution.py:17
  17.4 15.7 %all-to-all-start.2 = ((bf16[1,4,4,240,128]{4,2,1,0,3:T(4,128)(2,1)}), bf16[1,4,4,240,128]{4,2,1,0,3:T(4,128)(2,1)}, u32[]{:S(2)}, u32[]{:S(2)}) async-start(bf16[1,4,4,240,128]{4,2,1,0,3:T(4,128)(2,1)} %copy.31), calls=%async_computation.2 | async-start | bytes 1966080 | tf_op jit(solution)/shard_map/all_to_all | solution.py:76
  23.4 3.7 %copy-start.10 = (bf16[3,3,128,128]{3,2,1,0:T(8,128)(2,1)S(1)}, bf16[3,3,128,128]{3,2,1,0:T(8,128)(2,1)}, u32[]{:S(2)}) copy-start(bf16[3,3,128,128]{3,2,1,0:T(8,128)(2,1)} %param.6) | copy-start | bytes 884740
  34.5 0.9 copy-start.12
  37.6 16.7 %all-to-all-start.3 = ((bf16[1,8,4,120,128]{4,3,2,0,1:T(8,128)(2,1)}), bf16[1,8,4,120,128]{4,3,2,0,1:T(8,128)(2,1)}, u32[]{:S(2)}, u32[]{:S(2)}) async-start(bf16[1,8,4,120,128]{4,3,2,0,1:T(8,128)(2,1)} %bitcast.270), calls=%async_computation.3 | async-start | bytes 1966080 | tf_op jit(solution)/shard_map/all_to_all | solution.py:88
  54.4 1.8 copy-start
  57.0 1.2 copy-start.6
  57.0 1.2 copy-start.14
  57.0 1.3 copy-start.16
  68.0 25.4 %all-to-all-start = ((bf16[1,4,4,240,128]{4,2,1,0,3:T(4,128)(2,1)}), bf16[1,4,4,240,128]{4,2,1,0,3:T(4,128)(2,1)}, u32[]{:S(2)}, u32[]{:S(2)}) async-start(bf16[1,4,4,240,128]{4,2,1,0,3:T(4,128)(2,1)} %copy.26), calls=%async_computation | async-start | bytes 1966080 | tf_op jit(solution)/shard_map/all_to_all | solution.py:75
  72.5 121.8 %reduce-scatter.2.cloned.1.call-start = ((), (), s32[]{:S(2)}) async-start(), calls=%async_computation.5 | async-start | bytes 811008 | tf_op jit(solution)/shard_map/reduce_scatter | solution.py:117
  73.6 9.1 %collective-permute-start.2 = (bf16[1,4,1,240,128]{4,3,2,1,0:T(8,128)(2,1)S(1)}, bf16[1,4,1,240,128]{4,3,2,1,0:T(8,128)(2,1)S(1)}, u32[]{:S(2)}, u32[]{:S(2)}) collective-permute-start(bf16[1,4,1,240,128]{4,3,2,1,0:T(8,128)(2,1)S(1)} %get-tuple-element.23), channel_id=1, source_target_pairs={{0,1},{1,2},{2,3},{4,5},{5,6},{6,7},{8,9},{9,10},{10,11},{12,13},{... | collective-permute-start | bytes 737288 | tf_op jit(solution)/shard_map/ppermute | solution.py:16
  77.2 7.9 %collective-permute-start.3 = (bf16[1,4,1,240,128]{4,3,2,1,0:T(8,128)(2,1)S(1)}, bf16[1,4,1,240,128]{4,3,2,1,0:T(8,128)(2,1)S(1)}, u32[]{:S(2)}, u32[]{:S(2)}) collective-permute-start(bf16[1,4,1,240,128]{4,3,2,1,0:T(8,128)(2,1)S(1)} %get-tuple-element.24), channel_id=1, source_target_pairs={{1,0},{2,1},{3,2},{5,4},{6,5},{7,6},{9,8},{10,9},{11,10},{13,12},{... | collective-permute-start | bytes 737288 | tf_op jit(solution)/shard_map/ppermute | solution.py:17
  81.7 3.4 %copy-start.4 = (bf16[1,4,4,240,128]{4,3,2,1,0:T(8,128)(2,1)S(1)}, bf16[1,4,4,240,128]{4,3,2,1,0:T(8,128)(2,1)}, u32[]{:S(2)}) copy-start(bf16[1,4,4,240,128]{4,3,2,1,0:T(8,128)(2,1)} %get-tuple-element.3) | copy-start | bytes 2949124
  85.3 3.9 %copy-start.11 = (bf16[3,3,128,128]{3,2,1,0:T(8,128)(2,1)S(1)}, bf16[3,3,128,128]{3,2,1,0:T(8,128)(2,1)}, u32[]{:S(2)}) copy-start(bf16[3,3,128,128]{3,2,1,0:T(8,128)(2,1)} %param.6) | copy-start | bytes 884740
  97.8 1.1 copy-start.1
  100.4 1.2 copy-start.2
  103.0 4.5 %copy-start.3 = (f32[3840,128]{1,0:T(8,128)S(1)}, f32[3840,128]{1,0:T(8,128)}, u32[]{:S(2)}) copy-start(f32[3840,128]{1,0:T(8,128)} %convolution_add_fusion.2) | copy-start | bytes 5898244
  103.0 14.3 %all-to-all-start.1 = ((bf16[1,8,4,120,128]{4,3,2,0,1:T(8,128)(2,1)}), bf16[1,8,4,120,128]{4,3,2,0,1:T(8,128)(2,1)}, u32[]{:S(2)}, u32[]{:S(2)}) async-start(bf16[1,8,4,120,128]{4,3,2,0,1:T(8,128)(2,1)} %bitcast.271), calls=%async_computation.1 | async-start | bytes 1966080 | tf_op jit(solution)/shard_map/all_to_all | solution.py:87
  107.5 1.8 copy-start.8
  107.5 1.8 copy-start.9
  118.6 1.2 copy-start.7
  (2 other events, 1.4 us)
Sparse Core Ops, SparseCore 0:
  100.1 94.1 reduce-scatter.1
where the time goes:
time: 206 us; the launch traced here: 202 us
  waiting for transfers between devices  91.4 us (44%)
  matrix products  36.5 us (18%)
  starting transfers between devices  30.2 us (15%)
  local copies, waits for them, and re-layouts  23.1 us (11%)
  between operations  14.4 us (7%)
  other arithmetic  6.87 us (3%)
    reduce_scatter x1, waiting for transfers between devices, on_device(): lax.psum_scatter(partial_terms, ('dp', 'frame', 'row'), scatter_dimension...  73.3 us
    dot_general x12, matrix products, contract_rows(): lax.dot_general(left, right, (((0,), (0,)), ((), ())), preferred_element_...  15.9 us
    dot_general x9, matrix products, spatial_taps(): jnp.dot(piece, weights[i, j], preferred_element_type=jnp.float32)  8.81 us
    ppermute x2, starting transfers between devices, extended_2(): before = lax.ppermute(last, axis, up)  8.07 us
    all_to_all x1, waiting for transfers between devices, on_device(): lax.all_to_all(grad_act_band[None], 'frame', split_axis=1, concat_axis=3,...  7.43 us
    dot_general x9, matrix products, on_device(): jnp.dot(piece, spatial_weight[i, j].T, preferred_element_type=jnp.float32)  7.38 us
    unnamed x35, local copies, waits for them, and re-layouts  6.99 us
    all_to_all x1, waiting for transfers between devices, on_device(): lax.all_to_all(mixed_band[None], 'frame', split_axis=1, concat_axis=3, ti...  6.52 us
  transfers between devices with their start and end apart: 9, of which 5 were waited for; matrix products, arithmetic and copies ran while one was open for 18% of the time, Pallas kernels for 0%

commit v1 on v0

v1 whole, which is shorter than its diff:
```python
import functools
import math

import jax
import jax.numpy as jnp
from jax import lax
from jax.experimental import pallas as pl
from jax.experimental.pallas import tpu as pltpu
from jax.sharding import PartitionSpec as P

F32 = jnp.float32
BF16 = jnp.bfloat16
MESH = pl.DeviceIdType.MESH


def with_sides(value):
    width = value.shape[0]
    wide = value.astype(F32)
    place = lax.broadcasted_iota(jnp.int32, wide.shape, 0)
    before = jnp.where(place == 0, 0.0, pltpu.roll(wide, 1, 0)).astype(BF16)
    after = jnp.where(place == width - 1, 0.0, pltpu.roll(wide, width - 1, 0)).astype(BF16)
    return jnp.concatenate([before, value, after], axis=1)


def dot(left, right):
    return jnp.dot(left, right, preferred_element_type=F32)


def contract_rows(left, right):
    return lax.dot_general(left, right, (((0,), (0,)), ((), ())), preferred_element_type=F32)


def block_kernel(
    sizes, scale, x_hbm, g_hbm, sw, tw, y_hbm, dx_hbm, wg,
    xv, xh, xc, gv, ax, dv, ag, pc, pe, ph, wf, wb, tf, tb, acc, tacc, part, r1, s1, r2,
    yv, dxv, lsem, osem, xs, xr, cs, cr, as_, ar, ps, pr, s1s, s1r, s2s, s2r,
):
    nd, nf, nr = sizes
    frames, rows, width, chans = x_hbm.shape
    pairs, groups = rows // 2, frames // 2
    scatter = part is not None
    me_d, me_f, me_r = lax.axis_index("dp"), lax.axis_index("frame"), lax.axis_index("row")
    core = me_r % 2
    half = nr // 2
    chips = nd * nf * half
    me_q = (me_d * nf + me_f) * half + me_r // 2
    has_up, has_down = me_r > 0, me_r < nr - 1
    has_prev, has_next = me_f > 0, me_f < nf - 1

    def chip(q):
        return {"dp": q // (nf * half), "frame": (q // half) % nf, "row": 2 * (q % half) + core}

    def remote(src, dst, ssem, rsem, where):
        return pltpu.make_async_remote_copy(
            src_ref=src, dst_ref=dst, send_sem=ssem, recv_sem=rsem,
            device_id=where, device_id_type=MESH,
        )

    load_x = pltpu.make_async_copy(x_hbm, xv, lsem.at[0])
    load_g = pltpu.make_async_copy(g_hbm, gv.at[pl.ds(0, frames)], lsem.at[1])
    load_x.start()

    barrier = pltpu.get_barrier_semaphore()

    def greet(where):
        pl.semaphore_signal(barrier, inc=1, device_id=where, device_id_type=MESH)

    @pl.when(has_up)
    def _():
        greet({"row": me_r - 1})

    @pl.when(has_down)
    def _():
        greet({"row": me_r + 1})

    count = has_up.astype(jnp.int32) + has_down.astype(jnp.int32)
    if scatter:
        def greet_chip(o, carry):
            greet(chip((me_q + o) % chips))
            return carry

        lax.fori_loop(1, chips, greet_chip, 0)
        count = count + (chips - 1)
    else:
        @pl.when(has_prev)
        def _():
            greet({"frame": me_f - 1})

        @pl.when(has_next)
        def _():
            greet({"frame": me_f + 1})

        count = count + has_prev.astype(jnp.int32) + has_next.astype(jnp.int32)
    pl.semaphore_wait(barrier, count)

    x_up = remote(x_hbm.at[:, 0], xh.at[1], xs.at[0], xr.at[1], {"row": me_r - 1})
    x_down = remote(x_hbm.at[:, rows - 1], xh.at[0], xs.at[1], xr.at[0], {"row": me_r + 1})
    g_prev = remote(g_hbm.at[pl.ds(0, 2)], gv.at[pl.ds(frames, 2)], cs, cr, {"frame": me_f - 1})
    a_next = remote(ax.at[pl.ds(frames, 2)], ax.at[pl.ds(0, 2)], as_, ar, {"frame": me_f + 1})
    p_up = remote(pe.at[0], ph.at[1], ps.at[0], pr.at[1], {"row": me_r - 1})
    p_down = remote(pe.at[1], ph.at[0], ps.at[1], pr.at[0], {"row": me_r + 1})
    pl.when(has_up)(x_up.start)
    pl.when(has_down)(x_down.start)
    pl.when(has_prev)(g_prev.start)
    load_g.start()

    zero = jnp.zeros((chans, chans), BF16)
    for a in range(4):
        for b in range(2):
            i = a - b
            cols = pl.ds(b * chans, chans)
            for j in range(3):
                spot = pl.ds((a * 3 + j) * chans, chans)
                wf[spot, cols] = sw[i, j] if 0 <= i <= 2 else zero
                wb[spot, cols] = sw[2 - i, 2 - j].T if 0 <= i <= 2 else zero
            spot = pl.ds(a * chans, chans)
            k = b + 2 - a
            tf[spot, cols] = tw[k] if 0 <= k <= 2 else zero
            tb[spot, cols] = tw[i].T if 0 <= i <= 2 else zero

    load_x.wait()

    def widen(f, carry):
        for r in range(rows):
            xc[f, r + 1] = with_sides(xv[f, r])
        return carry

    lax.fori_loop(0, frames, widen, 0)

    def temporal_in(ref, f):
        return jnp.concatenate(
            [ref[f + a].reshape(rows * width, chans) for a in range(4)], axis=1
        )

    def act_grads(f):
        out = dot(temporal_in(gv, f), tb[...])
        for b in range(2):
            ag[f + b] = out[:, b * chans:(b + 1) * chans].astype(BF16).reshape(rows, width, chans)

    load_g.wait()
    for h in range(groups - 1):
        act_grads(2 * h)

    def halo(has, slot, src, dst, row, copy):
        @pl.when(has)
        def _():
            copy.wait_recv()

            def one(f, carry):
                dst[f, row] = with_sides(src[slot, f])
                return carry

            lax.fori_loop(0, frames, one, 0)

        @pl.when(jnp.logical_not(has))
        def _():
            def one(f, carry):
                dst[f, row] = jnp.zeros((width, 3 * chans), BF16)
                return carry

            lax.fori_loop(0, frames, one, 0)

    halo(has_up, 0, xh, xc, 0, x_down)
    halo(has_down, 1, xh, xc, rows + 1, x_up)

    def conv(src, weight, h, p):
        left = jnp.concatenate(
            [src[2 * h:2 * h + 2, 2 * p + a].reshape(2 * width, 3 * chans) for a in range(4)],
            axis=1,
        )
        return dot(left, weight[...])

    def forward(h):
        for p in range(pairs):
            pre = conv(xc, wf, h, p)
            for b in range(2):
                v = pre[:, b * chans:(b + 1) * chans]
                s = 0.5 + 0.5 * jnp.tanh(0.5 * v)
                shape = (2, width, chans)
                ax[2 * h + 2:2 * h + 4, 2 * p + b] = (v * s).astype(BF16).reshape(shape)
                dv[2 * h:2 * h + 2, 2 * p + b] = (s * (1.0 + v * (1.0 - s))).reshape(shape)

    forward(groups - 1)
    pl.when(has_next)(a_next.start)
    for h in range(groups - 1):
        forward(h)

    def pre_grads(h):
        def one(f, carry):
            for r in range(rows):
                v = (ag[f, r].astype(F32) * dv[f, r]).astype(BF16)
                pc[f, r + 1] = with_sides(v)
                if r == 0:
                    pe[0, f] = v
                if r == rows - 1:
                    pe[1, f] = v
            return carry

        lax.fori_loop(2 * h, 2 * h + 2, one, 0)

    def temporal_term(f):
        left = jnp.concatenate(
            [ax[f + 2 + a].reshape(rows * width, chans) for a in range(2)], axis=1
        )
        return contract_rows(left, temporal_in(gv, f))

    for h in range(groups - 1):
        pre_grads(h)
        if h == 0:
            tacc[...] = temporal_term(0)
        else:
            tacc[...] += temporal_term(2 * h)

    @pl.when(has_next)
    def _():
        g_prev.wait_recv()

    @pl.when(jnp.logical_not(has_next))
    def _():
        gv[frames:frames + 2] = jnp.zeros((2, rows, width, chans), BF16)

    act_grads(frames - 2)
    pre_grads(groups - 1)
    pl.when(has_up)(p_up.start)
    pl.when(has_down)(p_down.start)
    if groups > 1:
        tacc[...] += temporal_term(frames - 2)
    else:
        tacc[...] = temporal_term(frames - 2)

    for p in range(pairs):
        right = jnp.concatenate(
            [
                pc[:, 2 * p + 1 + b, :, chans:2 * chans].reshape(frames * width, chans)
                for b in range(2)
            ],
            axis=1,
        )
        for a in range(4):
            term = contract_rows(xc[:, 2 * p + a].reshape(frames * width, 3 * chans), right)
            if p == 0:
                acc[a] = term
            else:
                acc[a] += term

    def put(tap, value):
        if not scatter:
            wg[tap * chans:(tap + 1) * chans] = value
            return
        blocks = part.shape[2]
        for n in range(chans // 16):
            at = tap * (chans // 16) + n
            owner = at // blocks
            part[owner // 2, owner % 2, at % blocks] = value[n * 16:(n + 1) * 16]

    for i in range(3):
        for j in range(3):
            spot = pl.ds(j * chans, chans)
            put(i * 3 + j, acc[i, spot, 0:chans] + acc[i + 1, spot, chans:2 * chans])
    for k in range(3):
        total = None
        for a in range(2):
            piece = tacc[a * chans:(a + 1) * chans, (a + k) * chans:(a + k + 1) * chans]
            total = piece if total is None else total + piece
        put(9 + k, total)

    if scatter:
        core_copy = remote(part.at[:, 1 - core], r1, s1s, s1r, {"row": me_r + 1 - 2 * core})
        core_copy.start()

    def mix(h):
        out = dot(temporal_in(ax, 2 * h), tf[...])
        for b in range(2):
            f = 2 * h + b
            mixed = out[:, b * chans:(b + 1) * chans].astype(BF16).astype(F32)
            x = xc[f, 1:rows + 1, :, chans:2 * chans].reshape(rows * width, chans).astype(F32)
            yv[f] = (x + mixed).astype(BF16).reshape(rows, width, chans)
        spot = pl.ds(2 * h, 2)
        copy = pltpu.make_async_copy(yv.at[spot], y_hbm.at[spot], osem.at[h])
        copy.start()
        return copy

    outs = [mix(h) for h in range(1, groups)]

    if scatter:
        core_copy.wait_recv()

        def narrow(q, carry):
            s1[q] = (part[q, core] + r1[q]).astype(BF16)
            return carry

        lax.fori_loop(0, chips, narrow, 0)

        def to_chip(o):
            q = (me_q + o) % chips
            return remote(s1.at[q], r2.at[me_q], s2s.at[o], s2r.at[me_q], chip(q))

        def send(o, carry):
            to_chip(o).start()
            return carry

        lax.fori_loop(1, chips, send, 0)

    halo(has_up, 0, ph, pc, 0, p_down)
    halo(has_down, 1, ph, pc, rows + 1, p_up)
    for h in range(groups):
        for p in range(pairs):
            back = conv(pc, wb, h, p)
            for b in range(2):
                g = gv[2 * h:2 * h + 2, 2 * p + b].reshape(2 * width, chans).astype(F32)
                v = (g + back[:, b * chans:(b + 1) * chans]).astype(BF16)
                dxv[2 * h:2 * h + 2, 2 * p + b] = v.reshape(2, width, chans)
        spot = pl.ds(2 * h, 2)
        copy = pltpu.make_async_copy(dxv.at[spot], dx_hbm.at[spot], osem.at[groups + h])
        copy.start()
        outs.append(copy)

    @pl.when(has_prev)
    def _():
        a_next.wait_recv()

    @pl.when(jnp.logical_not(has_prev))
    def _():
        ax[0:2] = jnp.zeros((2, rows, width, chans), BF16)

    outs.append(mix(0))

    if scatter:
        wg[...] = (part[me_q, core] + r1[me_q]).reshape(wg.shape)

        def collect(o, carry):
            q = (me_q + chips - o) % chips
            remote(s1.at[q], r2.at[q], s2s.at[o], s2r.at[q], chip(q)).wait_recv()
            wg[...] += r2[q].astype(F32).reshape(wg.shape)
            to_chip(o).wait_send()
            return carry

        lax.fori_loop(1, chips, collect, 0)
        wg[...] = wg[...] * scale
        core_copy.wait_send()

    pl.when(has_up)(x_up.wait_send)
    pl.when(has_down)(x_down.wait_send)
    pl.when(has_prev)(g_prev.wait_send)
    pl.when(has_next)(a_next.wait_send)
    pl.when(has_up)(p_up.wait_send)
    pl.when(has_down)(p_down.wait_send)
    for copy in outs:
        copy.wait()


def on_device(sizes, clip_input, cotangent, spatial_weight, temporal_weight):
    x, g = clip_input[0], cotangent[0]
    frames, rows, width, chans = x.shape
    nd, nf, nr = sizes
    devices = nd * nf * nr
    scale = 1.0 / math.sqrt(nd * frames * nf * rows * nr * width)
    terms = 12 * chans
    own = terms // devices
    scatter = own % 16 == 0 and terms % devices == 0 and nr % 2 == 0
    chips = devices // 2
    blocks = own // 16
    dma, regular = pltpu.SemaphoreType.DMA, pltpu.VMEM
    scratch = [
        regular((frames, rows, width, chans), BF16),
        regular((2, frames, width, chans), BF16),
        regular((frames, rows + 2, width, 3 * chans), BF16),
        regular((frames + 2, rows, width, chans), BF16),
        regular((frames + 2, rows, width, chans), BF16),
        regular((frames, rows, width, chans), F32),
        regular((frames, rows, width, chans), BF16),
        regular((frames, rows + 2, width, 3 * chans), BF16),
        regular((2, frames, width, chans), BF16),
        regular((2, frames, width, chans), BF16),
        regular((12 * chans, 2 * chans), BF16),
        regular((12 * chans, 2 * chans), BF16),
        regular((4 * chans, 2 * chans), BF16),
        regular((4 * chans, 2 * chans), BF16),
        regular((4, 3 * chans, 2 * chans), F32),
        regular((2 * chans, 4 * chans), F32),
    ]
    if scatter:
        scratch += [
            regular((chips, 2, blocks, 16, chans), F32),
            regular((chips, blocks, 16, chans), F32),
            regular((chips, blocks, 16, chans), BF16),
            regular((chips, blocks, 16, chans), BF16),
        ]
    scratch += [
        regular((frames, rows, width, chans), BF16),
        regular((frames, rows, width, chans), BF16),
        dma((2,)), dma((frames,)),
        dma((2,)), dma((2,)), dma, dma, dma, dma, dma((2,)), dma((2,)),
    ]
    if scatter:
        scratch += [dma, dma, dma((chips,)), dma((chips,))]

    def kernel(*refs):
        refs = list(refs)
        if not scatter:
            refs[23:23] = [None] * 4
            refs += [None] * 4
        block_kernel(sizes, scale, *refs)

    whole = jax.ShapeDtypeStruct(x.shape, BF16)
    grads = jax.ShapeDtypeStruct((own if scatter else terms, chans), F32)
    anywhere = pl.BlockSpec(memory_space=pl.ANY)
    vmem = pl.BlockSpec(memory_space=pltpu.VMEM)
    y, dx, wg = pl.pallas_call(
        kernel,
        out_shape=(whole, whole, grads),
        in_specs=[anywhere, anywhere, vmem, vmem],
        out_specs=(anywhere, anywhere, vmem),
        scratch_shapes=scratch,
        compiler_params=pltpu.CompilerParams(
            collective_id=0, has_side_effects=True, vmem_limit_bytes=56 * 1024 * 1024
        ),
    )(x, g, spatial_weight, temporal_weight)
    if not scatter:
        wg = scale * lax.psum_scatter(
            wg, ("dp", "frame", "row"), scatter_dimension=0, tiled=True
        )
    return (y[None], dx[None], wg)


def solution(mesh):
    spread = P("dp", "frame", "row", None, None)
    sizes = tuple(mesh.shape[name] for name in ("dp", "frame", "row"))
    return jax.shard_map(
        functools.partial(on_device, sizes),
        mesh=mesh,
        in_specs=(spread, spread, P(), P()),
        out_specs=(spread, spread, P(("dp", "frame", "row"), None)),
        check_vma=False,
    )
```

time: 206 us -> 35.2 us (0.17); the launches traced: 202 us -> 35 us
  waiting for transfers between devices: 91.4 us -> 0 us
  matrix products: 36.5 us -> 0 us
  Pallas kernels: 0 us -> 30.5 us
  starting transfers between devices: 30.2 us -> 0 us
  local copies, waits for them, and re-layouts: 23.1 us -> 3.85 us
  between operations: 14.4 us -> 0.65 us
  other arithmetic: 6.87 us -> 0 us
    reduce_scatter x1 -> x0, waiting for transfers between devices: 73.3 us -> none  [on_device(): lax.psum_scatter(partial_terms, ('dp', 'frame', 'row'), scatter_dimension...]
    dot_general x36 -> x0, matrix products: 36.5 us -> none  [the longest x12 15.9 us: contract_rows(): lax.dot_general(left, right, (((0,), (0,)), ((), ())), preferred_element_...]
    pallas_call x0 -> x1, Pallas kernels: none -> 30.5 us  [on_device(): pl.pallas_call(kernel, out_shape=(whole, whole, grads), in_specs=[anywher...]
    all_to_all x4 -> x0, starting transfers between devices: 17.9 us -> none  [the longest x1 4.56 us: on_device(): lax.all_to_all(grad_act_band[None], 'frame', split_axis=1, concat_axis=3,...]
    all_to_all x4 -> x0, waiting for transfers between devices: 15.8 us -> none  [the longest x1 7.43 us: on_device(): lax.all_to_all(grad_act_band[None], 'frame', split_axis=1, concat_axis=3,...]
    ppermute x4 -> x0, starting transfers between devices: 12.3 us -> none  [the longest x2 8.07 us: extended_2(): before = lax.ppermute(last, axis, up)]
    slice x6 -> x0, local copies, waits for them, and re-layouts: 10.2 us -> none  [the longest x1 3.88 us: on_device(): gpad[:, 2 - i:2 - i + rows, 2 - j:2 - j + cols, :].reshape(-1, chans)]
    convert_element_type x4 -> x0, other arithmetic: 5.18 us -> none  [the longest x2 2.63 us: on_device(): (act_grad.astype(jnp.float32) * sigma * (1.0 + pre * (1.0 - sigma))).asty...]
  transfers between devices with their start and end apart: 9 -> 0, of which waited for: 5 -> 0; matrix products, arithmetic and copies ran while one was open for 18% -> 0% of each run, Pallas kernels for 0% -> 0%
where the time goes in v1:
time: 35.2 us; the launch traced here: 35 us
  Pallas kernels  30.5 us (87%)
  local copies, waits for them, and re-layouts  3.85 us (11%)
  between operations  0.65 us (2%)
    pallas_call x1, Pallas kernels, on_device(): pl.pallas_call(kernel, out_shape=(whole, whole, grads), in_specs=[anywher...  30.5 us
    unnamed x7, local copies, waits for them, and re-layouts  3.85 us

profile of v1, /device:TPU:1, one launch (start us, length us, event | category | flops | bytes accessed | tf_op | source)
XLA Modules:
  0.0 35.0 jit_solution(13604929840557218816)
XLA Ops:
  0.6 30.5 %shard_map.67 = (bf16[4,4,240,128]{3,2,1,0:T(8,128)(2,1)}, bf16[4,4,240,128]{3,2,1,0:T(8,128)(2,1)}, f32[48,128]{1,0:T(8,128)}) custom-call(bf16[4,4,240,128]{3,2,1,0:T(8,128)(2,1)} %bitcast.4, bf16[4,4,240,128]{3,2,1,0:T(8,128)(2,1)} %bitcast.5, bf16[3,3,128,128]{3,2,1,0:T(8,128)(2,1)} %refs_2_.1, bf16[3,128,128]{2,1,0:T(8,128)(2,1)} %refs_3_.1), custom_call_target="tpu_custom_call" | custom-call | tf_op jit(solution)/shard_map/pallas_call | solution.py:409
  31.1 0.0 copy-start
  31.1 2.3 %copy.10 = bf16[1,4,4,240,128]{4,3,2,1,0:T(8,128)(2,1)} copy(bf16[1,4,4,240,128]{4,3,2,1,0:T(8,128)(2,1)} %bitcast.7) | data formatting | bytes 1966080
  33.4 0.0 copy-done
  33.4 0.0 copy-start.1
  33.4 0.9 %copy.11 = bf16[1,4,4,240,128]{4,3,2,1,0:T(8,128)(2,1)} copy(bf16[1,4,4,240,128]{4,3,2,1,0:T(8,128)(2,1)S(1)} %bitcast.6) | data formatting | bytes 1966080
  34.4 0.0 copy-done.1
  34.4 0.6 %copy.12 = f32[48,128]{1,0:T(8,128)} copy(f32[48,128]{1,0:T(8,128)S(1)} %copy-done.1) | data formatting | bytes 49152
Async XLA Ops:
  31.1 2.3 %copy-start = (bf16[4,4,240,128]{3,2,1,0:T(8,128)(2,1)S(1)}, bf16[4,4,240,128]{3,2,1,0:T(8,128)(2,1)}, u32[]{:S(2)}) copy-start(bf16[4,4,240,128]{3,2,1,0:T(8,128)(2,1)} %get-tuple-element.7) | copy-start | bytes 2949124
  33.4 0.9 %copy-start.1 = (f32[48,128]{1,0:T(8,128)S(1)}, f32[48,128]{1,0:T(8,128)}, u32[]{:S(2)}) copy-start(f32[48,128]{1,0:T(8,128)} %get-tuple-element.14) | copy-start | bytes 73732

commit v2 on v1

--- a/solution.py
+++ b/solution.py
@@ -95,13 +95,27 @@
 
     x_up = remote(x_hbm.at[:, 0], xh.at[1], xs.at[0], xr.at[1], {"row": me_r - 1})
     x_down = remote(x_hbm.at[:, rows - 1], xh.at[0], xs.at[1], xr.at[0], {"row": me_r + 1})
-    g_prev = remote(g_hbm.at[pl.ds(0, 2)], gv.at[pl.ds(frames, 2)], cs, cr, {"frame": me_f - 1})
+    g_prev = [
+        remote(
+            g_hbm.at[pl.ds(0, 2), pl.ds(2 * p, 2)], gv.at[pl.ds(frames, 2), pl.ds(2 * p, 2)],
+            cs.at[p], cr.at[p], {"frame": me_f - 1},
+        )
+        for p in range(pairs)
+    ]
     a_next = remote(ax.at[pl.ds(frames, 2)], ax.at[pl.ds(0, 2)], as_, ar, {"frame": me_f + 1})
-    p_up = remote(pe.at[0], ph.at[1], ps.at[0], pr.at[1], {"row": me_r - 1})
-    p_down = remote(pe.at[1], ph.at[0], ps.at[1], pr.at[0], {"row": me_r + 1})
+    p_up, p_down = [], []
+    for h in range(groups):
+        spot = pl.ds(2 * h, 2)
+        p_up.append(remote(
+            pe.at[0, spot], ph.at[1, spot], ps.at[0, h], pr.at[1, h], {"row": me_r - 1}
+        ))
+        p_down.append(remote(
+            pe.at[1, spot], ph.at[0, spot], ps.at[1, h], pr.at[0, h], {"row": me_r + 1}
+        ))
     pl.when(has_up)(x_up.start)
     pl.when(has_down)(x_down.start)
-    pl.when(has_prev)(g_prev.start)
+    for copy in g_prev:
+        pl.when(has_prev)(copy.start)
     load_g.start()
 
     zero = jnp.zeros((chans, chans), BF16)
@@ -127,21 +141,22 @@
 
     lax.fori_loop(0, frames, widen, 0)
 
-    def temporal_in(ref, f):
+    def temporal_in(ref, f, lo, hi):
         return jnp.concatenate(
-            [ref[f + a].reshape(rows * width, chans) for a in range(4)], axis=1
-        )
-
-    def act_grads(f):
-        out = dot(temporal_in(gv, f), tb[...])
+            [ref[f + a, lo:hi].reshape((hi - lo) * width, chans) for a in range(4)], axis=1
+        )
+
+    def act_grads(f, lo, hi):
+        out = dot(temporal_in(gv, f, lo, hi), tb[...])
         for b in range(2):
-            ag[f + b] = out[:, b * chans:(b + 1) * chans].astype(BF16).reshape(rows, width, chans)
+            v = out[:, b * chans:(b + 1) * chans].astype(BF16)
+            ag[f + b, lo:hi] = v.reshape(hi - lo, width, chans)
 
     load_g.wait()
     for h in range(groups - 1):
-        act_grads(2 * h)
-
-    def halo(has, slot, src, dst, row, copy):
+        act_grads(2 * h, 0, rows)
+
+    def halo(has, slot, src, dst, row, copy, first, last):
         @pl.when(has)
         def _():
             copy.wait_recv()
@@ -150,7 +165,7 @@
                 dst[f, row] = with_sides(src[slot, f])
                 return carry
 
-            lax.fori_loop(0, frames, one, 0)
+            lax.fori_loop(first, last, one, 0)
 
         @pl.when(jnp.logical_not(has))
         def _():
@@ -158,10 +173,10 @@
                 dst[f, row] = jnp.zeros((width, 3 * chans), BF16)
                 return carry
 
-            lax.fori_loop(0, frames, one, 0)
-
-    halo(has_up, 0, xh, xc, 0, x_down)
-    halo(has_down, 1, xh, xc, rows + 1, x_up)
+            lax.fori_loop(first, last, one, 0)
+
+    halo(has_up, 0, xh, xc, 0, x_down, 0, frames)
+    halo(has_down, 1, xh, xc, rows + 1, x_up, 0, frames)
 
     def conv(src, weight, h, p):
         left = jnp.concatenate(
@@ -185,9 +200,9 @@
     for h in range(groups - 1):
         forward(h)
 
-    def pre_grads(h):
+    def pre_grads(h, lo, hi):
         def one(f, carry):
-            for r in range(rows):
+            for r in range(lo, hi):
                 v = (ag[f, r].astype(F32) * dv[f, r]).astype(BF16)
                 pc[f, r + 1] = with_sides(v)
                 if r == 0:
@@ -198,50 +213,92 @@
 
         lax.fori_loop(2 * h, 2 * h + 2, one, 0)
 
-    def temporal_term(f):
+    def temporal_term(h, lo, hi, fresh):
+        f = 2 * h
         left = jnp.concatenate(
-            [ax[f + 2 + a].reshape(rows * width, chans) for a in range(2)], axis=1
-        )
-        return contract_rows(left, temporal_in(gv, f))
-
-    for h in range(groups - 1):
-        pre_grads(h)
-        if h == 0:
-            tacc[...] = temporal_term(0)
+            [ax[f + 2 + a, lo:hi].reshape((hi - lo) * width, chans) for a in range(2)], axis=1
+        )
+        term = contract_rows(left, temporal_in(gv, f, lo, hi))
+        if fresh:
+            tacc[...] = term
         else:
-            tacc[...] += temporal_term(2 * h)
-
-    @pl.when(has_next)
-    def _():
-        g_prev.wait_recv()
-
-    @pl.when(jnp.logical_not(has_next))
-    def _():
-        gv[frames:frames + 2] = jnp.zeros((2, rows, width, chans), BF16)
-
-    act_grads(frames - 2)
-    pre_grads(groups - 1)
-    pl.when(has_up)(p_up.start)
-    pl.when(has_down)(p_down.start)
-    if groups > 1:
-        tacc[...] += temporal_term(frames - 2)
-    else:
-        tacc[...] = temporal_term(frames - 2)
-
-    for p in range(pairs):
+            tacc[...] += term
+
+    def spatial_term(h, p, fresh):
         right = jnp.concatenate(
             [
-                pc[:, 2 * p + 1 + b, :, chans:2 * chans].reshape(frames * width, chans)
+                pc[2 * h:2 * h + 2, 2 * p + 1 + b, :, chans:2 * chans].reshape(2 * width, chans)
                 for b in range(2)
             ],
             axis=1,
         )
         for a in range(4):
-            term = contract_rows(xc[:, 2 * p + a].reshape(frames * width, 3 * chans), right)
-            if p == 0:
+            left = xc[2 * h:2 * h + 2, 2 * p + a].reshape(2 * width, 3 * chans)
+            term = contract_rows(left, right)
+            if fresh:
                 acc[a] = term
             else:
                 acc[a] += term
+
+    def send_edges(h):
+        pl.when(has_up)(p_up[h].start)
+        pl.when(has_down)(p_down[h].start)
+
+    def mix(h):
+        out = dot(temporal_in(ax, 2 * h, 0, rows), tf[...])
+        for b in range(2):
+            f = 2 * h + b
+            mixed = out[:, b * chans:(b + 1) * chans].astype(BF16).astype(F32)
+            x = xc[f, 1:rows + 1, :, chans:2 * chans].reshape(rows * width, chans).astype(F32)
+            yv[f] = (x + mixed).astype(BF16).reshape(rows, width, chans)
+        spot = pl.ds(2 * h, 2)
+        copy = pltpu.make_async_copy(yv.at[spot], y_hbm.at[spot], osem.at[h])
+        copy.start()
+        return copy
+
+    def backward(h):
+        halo(has_up, 0, ph, pc, 0, p_down[h], 2 * h, 2 * h + 2)
+        halo(has_down, 1, ph, pc, rows + 1, p_up[h], 2 * h, 2 * h + 2)
+        for p in range(pairs):
+            back = conv(pc, wb, h, p)
+            for b in range(2):
+                g = gv[2 * h:2 * h + 2, 2 * p + b].reshape(2 * width, chans).astype(F32)
+                v = (g + back[:, b * chans:(b + 1) * chans]).astype(BF16)
+                dxv[2 * h:2 * h + 2, 2 * p + b] = v.reshape(2, width, chans)
+        spot = pl.ds(2 * h, 2)
+        copy = pltpu.make_async_copy(dxv.at[spot], dx_hbm.at[spot], osem.at[groups + h])
+        copy.start()
+        return copy
+
+    outs = []
+    for h in range(groups - 1):
+        pre_grads(h, 0, rows)
+        send_edges(h)
+        temporal_term(h, 0, rows, h == 0)
+        for p in range(pairs):
+            spatial_term(h, p, h == 0 and p == 0)
+    for h in range(1, groups):
+        outs.append(mix(h))
+    for h in range(groups - 1):
+        outs.append(backward(h))
+
+    for p in range(pairs):
+        lo, hi = 2 * p, 2 * p + 2
+
+        @pl.when(has_next)
+        def _():
+            g_prev[p].wait_recv()
+
+        @pl.when(jnp.logical_not(has_next))
+        def _():
+            gv[frames:frames + 2, lo:hi] = jnp.zeros((2, 2, width, chans), BF16)
+
+        act_grads(frames - 2, lo, hi)
+        pre_grads(groups - 1, lo, hi)
+        if p == pairs - 1:
+            send_edges(groups - 1)
+        temporal_term(groups - 1, lo, hi, groups == 1 and p == 0)
+        spatial_term(groups - 1, p, groups == 1 and p == 0)
 
     def put(tap, value):
         if not scatter:
@@ -268,20 +325,6 @@
         core_copy = remote(part.at[:, 1 - core], r1, s1s, s1r, {"row": me_r + 1 - 2 * core})
         core_copy.start()
 
-    def mix(h):
-        out = dot(temporal_in(ax, 2 * h), tf[...])
-        for b in range(2):
-            f = 2 * h + b
-            mixed = out[:, b * chans:(b + 1) * chans].astype(BF16).astype(F32)
-            x = xc[f, 1:rows + 1, :, chans:2 * chans].reshape(rows * width, chans).astype(F32)
-            yv[f] = (x + mixed).astype(BF16).reshape(rows, width, chans)
-        spot = pl.ds(2 * h, 2)
-        copy = pltpu.make_async_copy(yv.at[spot], y_hbm.at[spot], osem.at[h])
-        copy.start()
-        return copy
-
-    outs = [mix(h) for h in range(1, groups)]
-
     if scatter:
         core_copy.wait_recv()
 
@@ -301,19 +344,7 @@
 
         lax.fori_loop(1, chips, send, 0)
 
-    halo(has_up, 0, ph, pc, 0, p_down)
-    halo(has_down, 1, ph, pc, rows + 1, p_up)
-    for h in range(groups):
-        for p in range(pairs):
-            back = conv(pc, wb, h, p)
-            for b in range(2):
-                g = gv[2 * h:2 * h + 2, 2 * p + b].reshape(2 * width, chans).astype(F32)
-                v = (g + back[:, b * chans:(b + 1) * chans]).astype(BF16)
-                dxv[2 * h:2 * h + 2, 2 * p + b] = v.reshape(2, width, chans)
-        spot = pl.ds(2 * h, 2)
-        copy = pltpu.make_async_copy(dxv.at[spot], dx_hbm.at[spot], osem.at[groups + h])
-        copy.start()
-        outs.append(copy)
+    outs.append(backward(groups - 1))
 
     @pl.when(has_prev)
     def _():
@@ -341,10 +372,12 @@
 
     pl.when(has_up)(x_up.wait_send)
     pl.when(has_down)(x_down.wait_send)
-    pl.when(has_prev)(g_prev.wait_send)
+    for copy in g_prev:
+        pl.when(has_prev)(copy.wait_send)
     pl.when(has_next)(a_next.wait_send)
-    pl.when(has_up)(p_up.wait_send)
-    pl.when(has_down)(p_down.wait_send)
+    for h in range(groups):
+        pl.when(has_up)(p_up[h].wait_send)
+        pl.when(has_down)(p_down[h].wait_send)
     for copy in outs:
         copy.wait()
 
@@ -390,7 +423,8 @@
         regular((frames, rows, width, chans), BF16),
         regular((frames, rows, width, chans), BF16),
         dma((2,)), dma((frames,)),
-        dma((2,)), dma((2,)), dma, dma, dma, dma, dma((2,)), dma((2,)),
+        dma((2,)), dma((2,)), dma((rows // 2,)), dma((rows // 2,)), dma, dma,
+        dma((2, frames // 2)), dma((2, frames // 2)),
     ]
     if scatter:
         scratch += [dma, dma, dma((chips,)), dma((chips,))]

time: 35.2 us -> 35.5 us (level)
  no operation moved by 1% of the time
where the time goes in v2:
time: 35.5 us; the launch traced here: 35.2 us
  Pallas kernels  30.7 us (86%)
  local copies, waits for them, and re-layouts  3.85 us (11%)
  between operations  0.65 us (2%)
    pallas_call x1, Pallas kernels, on_device(): pl.pallas_call(kernel, out_shape=(whole, whole, grads), in_specs=[anywher...  30.7 us
    unnamed x7, local copies, waits for them, and re-layouts  3.85 us

profile of v2, /device:TPU:1, one launch (start us, length us, event | category | flops | bytes accessed | tf_op | source)
XLA Modules:
  0.0 35.2 jit_solution(17393105797548352438)
XLA Ops:
  0.6 30.7 %shard_map.67 = (bf16[4,4,240,128]{3,2,1,0:T(8,128)(2,1)}, bf16[4,4,240,128]{3,2,1,0:T(8,128)(2,1)}, f32[48,128]{1,0:T(8,128)}) custom-call(bf16[4,4,240,128]{3,2,1,0:T(8,128)(2,1)} %bitcast.4, bf16[4,4,240,128]{3,2,1,0:T(8,128)(2,1)} %bitcast.5, bf16[3,3,128,128]{3,2,1,0:T(8,128)(2,1)} %refs_2_.1, bf16[3,128,128]{2,1,0:T(8,128)(2,1)} %refs_3_.1), custom_call_target="tpu_custom_call" | custom-call | tf_op jit(solution)/shard_map/pallas_call | solution.py:443
  31.4 0.0 copy-start
  31.4 2.3 %copy.10 = bf16[1,4,4,240,128]{4,3,2,1,0:T(8,128)(2,1)} copy(bf16[1,4,4,240,128]{4,3,2,1,0:T(8,128)(2,1)} %bitcast.7) | data formatting | bytes 1966080
  33.7 0.0 copy-done
  33.7 0.0 copy-start.1
  33.7 0.9 %copy.11 = bf16[1,4,4,240,128]{4,3,2,1,0:T(8,128)(2,1)} copy(bf16[1,4,4,240,128]{4,3,2,1,0:T(8,128)(2,1)S(1)} %bitcast.6) | data formatting | bytes 1966080
  34.6 0.0 copy-done.1
  34.6 0.6 %copy.12 = f32[48,128]{1,0:T(8,128)} copy(f32[48,128]{1,0:T(8,128)S(1)} %copy-done.1) | data formatting | bytes 49152
Async XLA Ops:
  31.4 2.3 %copy-start = (bf16[4,4,240,128]{3,2,1,0:T(8,128)(2,1)S(1)}, bf16[4,4,240,128]{3,2,1,0:T(8,128)(2,1)}, u32[]{:S(2)}) copy-start(bf16[4,4,240,128]{3,2,1,0:T(8,128)(2,1)} %get-tuple-element.7) | copy-start | bytes 2949124
  33.7 0.9 %copy-start.1 = (f32[48,128]{1,0:T(8,128)S(1)}, f32[48,128]{1,0:T(8,128)}, u32[]{:S(2)}) copy-start(f32[48,128]{1,0:T(8,128)} %get-tuple-element.14) | copy-start | bytes 73732

commit v3 on v2

--- a/solution.py
+++ b/solution.py
@@ -33,7 +33,7 @@
 def block_kernel(
     sizes, scale, x_hbm, g_hbm, sw, tw, y_hbm, dx_hbm, wg,
     xv, xh, xc, gv, ax, dv, ag, pc, pe, ph, wf, wb, tf, tb, acc, tacc, part, r1, s1, r2,
-    yv, dxv, lsem, osem, xs, xr, cs, cr, as_, ar, ps, pr, s1s, s1r, s2s, s2r,
+    s3, r3, yv, dxv, lsem, osem, xs, xr, cs, cr, as_, ar, ps, pr, s1s, s1r, s2s, s2r, s3s, s3r,
 ):
     nd, nf, nr = sizes
     frames, rows, width, chans = x_hbm.shape
@@ -43,12 +43,14 @@
     core = me_r % 2
     half = nr // 2
     chips = nd * nf * half
-    me_q = (me_d * nf + me_f) * half + me_r // 2
+    plane = nf * half
+    me_p = me_f * half + me_r // 2
+    me_q = me_d * plane + me_p
     has_up, has_down = me_r > 0, me_r < nr - 1
     has_prev, has_next = me_f > 0, me_f < nf - 1
 
-    def chip(q):
-        return {"dp": q // (nf * half), "frame": (q // half) % nf, "row": 2 * (q % half) + core}
+    def chip(p):
+        return {"frame": p // half, "row": 2 * (p % half) + core}
 
     def remote(src, dst, ssem, rsem, where):
         return pltpu.make_async_remote_copy(
@@ -76,11 +78,13 @@
     count = has_up.astype(jnp.int32) + has_down.astype(jnp.int32)
     if scatter:
         def greet_chip(o, carry):
-            greet(chip((me_q + o) % chips))
+            greet(chip((me_p + o) % plane))
             return carry
 
-        lax.fori_loop(1, chips, greet_chip, 0)
-        count = count + (chips - 1)
+        lax.fori_loop(1, plane, greet_chip, 0)
+        for o in range(1, nd):
+            greet({"dp": (me_d + o) % nd})
+        count = count + (plane - 1) + (nd - 1)
     else:
         @pl.when(has_prev)
         def _():
@@ -329,22 +333,40 @@
         core_copy.wait_recv()
 
         def narrow(q, carry):
-            s1[q] = (part[q, core] + r1[q]).astype(BF16)
+            s1[q % plane, q // plane] = (part[q, core] + r1[q]).astype(BF16)
             return carry
 
         lax.fori_loop(0, chips, narrow, 0)
 
-        def to_chip(o):
-            q = (me_q + o) % chips
-            return remote(s1.at[q], r2.at[me_q], s2s.at[o], s2r.at[me_q], chip(q))
-
-        def send(o, carry):
-            to_chip(o).start()
+        def in_plane(o):
+            p = (me_p + o) % plane
+            return remote(s1.at[p], r2.at[me_p], s2s.at[o], s2r.at[me_p], chip(p))
+
+        for o in range(1, plane):
+            in_plane(o).start()
+
+    outs.append(backward(groups - 1))
+
+    if scatter:
+        for o in range(1, plane):
+            p = (me_p + plane - o) % plane
+            remote(s1.at[p], r2.at[p], s2s.at[o], s2r.at[p], chip(p)).wait_recv()
+
+        def gather(d, carry):
+            total = part[d * plane + me_p, core] + r1[d * plane + me_p]
+            for o in range(1, plane):
+                total = total + r2[(me_p + plane - o) % plane, d].astype(F32)
+            s3[d] = total
             return carry
 
-        lax.fori_loop(1, chips, send, 0)
-
-    outs.append(backward(groups - 1))
+        lax.fori_loop(0, nd, gather, 0)
+
+        def along_dp(o):
+            d = (me_d + o) % nd
+            return remote(s3.at[d], r3.at[me_d], s3s.at[o], s3r.at[me_d], {"dp": d})
+
+        for o in range(1, nd):
+            along_dp(o).start()
 
     @pl.when(has_prev)
     def _():
@@ -357,17 +379,15 @@
     outs.append(mix(0))
 
     if scatter:
-        wg[...] = (part[me_q, core] + r1[me_q]).reshape(wg.shape)
-
-        def collect(o, carry):
-            q = (me_q + chips - o) % chips
-            remote(s1.at[q], r2.at[q], s2s.at[o], s2r.at[q], chip(q)).wait_recv()
-            wg[...] += r2[q].astype(F32).reshape(wg.shape)
-            to_chip(o).wait_send()
-            return carry
-
-        lax.fori_loop(1, chips, collect, 0)
+        wg[...] = s3[me_d].reshape(wg.shape)
+        for o in range(1, nd):
+            d = (me_d + nd - o) % nd
+            remote(s3.at[d], r3.at[d], s3s.at[o], s3r.at[d], {"dp": d}).wait_recv()
+            wg[...] += r3[d].reshape(wg.shape)
+            along_dp(o).wait_send()
         wg[...] = wg[...] * scale
+        for o in range(1, plane):
+            in_plane(o).wait_send()
         core_copy.wait_send()
 
     pl.when(has_up)(x_up.wait_send)
@@ -416,8 +436,10 @@
         scratch += [
             regular((chips, 2, blocks, 16, chans), F32),
             regular((chips, blocks, 16, chans), F32),
-            regular((chips, blocks, 16, chans), BF16),
-            regular((chips, blocks, 16, chans), BF16),
+            regular((chips // nd, nd, blocks, 16, chans), BF16),
+            regular((chips // nd, nd, blocks, 16, chans), BF16),
+            regular((nd, blocks, 16, chans), F32),
+            regular((nd, blocks, 16, chans), F32),
         ]
     scratch += [
         regular((frames, rows, width, chans), BF16),
@@ -427,13 +449,13 @@
         dma((2, frames // 2)), dma((2, frames // 2)),
     ]
     if scatter:
-        scratch += [dma, dma, dma((chips,)), dma((chips,))]
+        scratch += [dma, dma, dma((chips // nd,)), dma((chips // nd,)), dma((nd,)), dma((nd,))]
 
     def kernel(*refs):
         refs = list(refs)
         if not scatter:
-            refs[23:23] = [None] * 4
-            refs += [None] * 4
+            refs[23:23] = [None] * 6
+            refs += [None] * 6
         block_kernel(sizes, scale, *refs)
 
     whole = jax.ShapeDtypeStruct(x.shape, BF16)

time: 35.5 us -> 36 us (1.014)
  the two profiles are of different devices: /device:TPU:1 before, /device:TPU:0 now
where the time goes in v3:
time: 36 us; the launch traced here: 35.8 us
  Pallas kernels  31.3 us (87%)
  local copies, waits for them, and re-layouts  3.85 us (11%)
  between operations  0.65 us (2%)
    pallas_call x1, Pallas kernels, on_device(): pl.pallas_call(kernel, out_shape=(whole, whole, grads), in_specs=[anywher...  31.3 us
    unnamed x7, local copies, waits for them, and re-layouts  3.85 us

profile of v3, /device:TPU:0, one launch (start us, length us, event | category | flops | bytes accessed | tf_op | source)
XLA Modules:
  0.0 35.8 jit_solution(14752786822205074304)
XLA Ops:
  0.6 31.3 %shard_map.67 = (bf16[4,4,240,128]{3,2,1,0:T(8,128)(2,1)}, bf16[4,4,240,128]{3,2,1,0:T(8,128)(2,1)}, f32[48,128]{1,0:T(8,128)}) custom-call(bf16[4,4,240,128]{3,2,1,0:T(8,128)(2,1)} %bitcast.4, bf16[4,4,240,128]{3,2,1,0:T(8,128)(2,1)} %bitcast.5, bf16[3,3,128,128]{3,2,1,0:T(8,128)(2,1)} %refs_2_.1, bf16[3,128,128]{2,1,0:T(8,128)(2,1)} %refs_3_.1), custom_call_target="tpu_custom_call" | custom-call | tf_op jit(solution)/shard_map/pallas_call | solution.py:465
  31.9 0.0 copy-start
  32.0 2.3 %copy.10 = bf16[1,4,4,240,128]{4,3,2,1,0:T(8,128)(2,1)} copy(bf16[1,4,4,240,128]{4,3,2,1,0:T(8,128)(2,1)} %bitcast.7) | data formatting | bytes 1966080
  34.3 0.0 copy-done
  34.3 0.0 copy-start.1
  34.3 0.9 %copy.11 = bf16[1,4,4,240,128]{4,3,2,1,0:T(8,128)(2,1)} copy(bf16[1,4,4,240,128]{4,3,2,1,0:T(8,128)(2,1)S(1)} %bitcast.6) | data formatting | bytes 1966080
  35.2 0.0 copy-done.1
  35.2 0.6 %copy.12 = f32[48,128]{1,0:T(8,128)} copy(f32[48,128]{1,0:T(8,128)S(1)} %copy-done.1) | data formatting | bytes 49152
Async XLA Ops:
  31.9 2.3 %copy-start = (bf16[4,4,240,128]{3,2,1,0:T(8,128)(2,1)S(1)}, bf16[4,4,240,128]{3,2,1,0:T(8,128)(2,1)}, u32[]{:S(2)}) copy-start(bf16[4,4,240,128]{3,2,1,0:T(8,128)(2,1)} %get-tuple-element.7) | copy-start | bytes 2949124
  34.3 0.9 %copy-start.1 = (f32[48,128]{1,0:T(8,128)S(1)}, f32[48,128]{1,0:T(8,128)}, u32[]{:S(2)}) copy-start(f32[48,128]{1,0:T(8,128)} %get-tuple-element.14) | copy-start | bytes 73732
